TPU v7x, 32 devices: a whole 2x2x4 slice. The times are simulated.
32 devices in a mesh: cube: 8 (over y, x, core), grid: 4 (over z).
Axes of the slice: x: 2, y: 2, z: 4, core: 2. Of those that a mesh axis runs over, the one named last changes fastest.
Arguments:
- child_update: bfloat16 [512, 2048], P('cube', 'grid'), may hold values from -6 to 6
- child_panel: bfloat16 [512, 512], P('grid', 'cube'), may hold values from -6 to 6
- panel_entries: bfloat16 [512, 4096], P('grid', 'cube'), may hold values from -6 to 6
- panel_inverse: bfloat16 [512, 512], replicated, as said below
- block_owner: int32 [128], replicated, may hold values from 0 to 7, as said below
- child_dest: int32 [32], replicated, may hold values from 0 to 127, as said below
- child_rows: int32 [32, 16], P('cube'), may hold values from 0 to 15, each once within a row
Outputs:
- schur_update: bfloat16 [4096, 2048], P('cube', 'grid')
- panel_factor: bfloat16 [512, 4096], P('grid', 'cube')
Inputs may be any that keep to these rules, and one draw needn't show every extreme that they name: `block_owner`: row blocks r*32 to (r+1)*32 - 1 form column range r. One cube index owns at most 8 row blocks of one range, and in every draw some cube index owns exactly 8 of some range. Every cube index owns at least one row block. `child_dest`: entry s*4+k names the parent row block into which child row block k of cube index s adds. The 4 child row blocks of one cube index go to blocks of 4 different owners, and in every draw some owner receives a block from every cube index. `panel_inverse`: zero below the diagonal, positive on it.
All inputs are finite; a program needn't handle non-finite values.
Results may differ from a plain program's by a relative error of at most 0.0057.
Values may be sent and summed in bfloat16 or wider, within the bound.
No kernel may reach another device: no remote copies, remote signals or barrier semaphores. Data moves between devices by JAX's collectives and lax.ppermute only.
A program may use at most 64 MiB of HBM per device.

v0:
```python
import functools

import jax
import jax.numpy as jnp
from jax import lax
from jax.experimental import pallas as pl
from jax.experimental.pallas import tpu as pltpu
from jax.sharding import PartitionSpec as P

F32 = jnp.float32
BF16 = jnp.bfloat16
I32 = jnp.int32
VMEM = pl.BlockSpec(memory_space=pltpu.VMEM)
SMEM = pl.BlockSpec(memory_space=pltpu.SMEM)
ANY = pl.BlockSpec(memory_space=pl.ANY)
MIB = 1024 * 1024
JOIN_COST = 1500000000


def call(body, outs, in_specs, scratch, flops, moved, out_specs=None, limit=16, aliases={}):
    return pl.pallas_call(
        body,
        out_shape=outs,
        in_specs=in_specs,
        out_specs=[VMEM] * len(outs) if out_specs is None else out_specs,
        scratch_shapes=scratch,
        input_output_aliases=aliases,
        compiler_params=pltpu.CompilerParams(vmem_limit_bytes=limit * MIB),
        cost_estimate=pl.CostEstimate(flops=flops, bytes_accessed=moved, transcendentals=0),
    )


def rows_at(index, size):
    return pl.ds(pl.multiple_of(index * size, size), size)


def first_body(grids, span, rows_hbm, panel_hbm, entries_hbm, *refs):
    firsts, flipped = refs[:grids], refs[grids]
    rows_ref, panel_ref, entries_ref, sems = refs[grids + 1 :]
    copies = [
        pltpu.make_async_copy(source, target, sems.at[i])
        for i, (source, target) in enumerate(
            ((entries_hbm, entries_ref), (panel_hbm, panel_ref), (rows_hbm, rows_ref))
        )
    ]
    for copy in copies:
        copy.start()
    column = lax.axis_index("grid")
    children, rows = rows_ref.shape
    copies[0].wait()
    flipped[...] = entries_ref[...].astype(F32).T.astype(BF16)
    for d in range(grids):
        firsts[d][pl.ds(0, span), :] = flipped[rows_at(jnp.bitwise_xor(column, d), span), :]
    for copy in copies[1:]:
        copy.wait()
    for k in range(children):
        want = rows_ref[k : k + 1, :]
        put = (lax.broadcasted_iota(I32, (rows, rows), 0) == want).astype(BF16)
        part = pl.ds(k * rows, rows)
        placed = jnp.dot(put, panel_ref[part, :], preferred_element_type=F32).astype(BF16)
        for d in range(grids):
            firsts[d][pl.ds(span + k * rows, rows), :] = placed


def second_body(
    cubes, grids, span, owner_hbm, dest_hbm, rows_hbm, update_hbm, inverse_hbm, flipped, *refs
):
    rests, blocks_ref, turned_ref = refs[:grids], *refs[grids : grids + 2]
    owner_ref, dest_ref, rows_ref, update_ref, sems = refs[grids + 2 :]
    copies = [
        pltpu.make_async_copy(source, target, sems.at[i])
        for i, (source, target) in enumerate(
            (
                (rows_hbm, rows_ref),
                (update_hbm, update_ref),
                (owner_hbm, owner_ref),
                (dest_hbm, dest_ref),
            )
        )
    ]
    mine = lax.axis_index("cube")
    column = lax.axis_index("grid")
    depth = flipped.shape[1]
    for d in range(grids):
        part = inverse_hbm.at[rows_at(jnp.bitwise_xor(column, d), depth), :]
        copies.append(pltpu.make_async_copy(part, turned_ref.at[pl.ds(d * depth, depth), :], sems.at[4 + d]))
    for copy in copies:
        copy.start()
    children, rows = rows_ref.shape
    blocks_ref[...] = jnp.zeros_like(blocks_ref)
    for d in range(grids):
        piece = flipped[rows_at(jnp.bitwise_xor(column, d), span), :]
        for e in range(grids):
            if e != d:
                k = d if d < e else d - 1
                rests[e][pl.ds(k * span, span), :] = piece
    for copy in copies[:4]:
        copy.wait()
    for k in range(children):
        want = rows_ref[k : k + 1, :]
        put = (lax.broadcasted_iota(I32, (rows, rows), 0) == want).astype(BF16)
        part = pl.ds(k * rows, rows)
        moved = jnp.dot(put, update_ref[part, :], preferred_element_type=F32).astype(BF16)
        d = jnp.bitwise_xor(owner_ref[dest_ref[mine * children + k]], mine)
        blocks_ref[rows_at(d, rows), :] = moved
    for copy in copies[4:]:
        copy.wait()


def pack_body(parts, rows, base, blocks_ref, *refs):
    firsts, payloads = refs[: len(parts)], refs[len(parts) :]
    depth = firsts[0].shape[1]
    panel = payloads[0].shape[1]
    chunks = blocks_ref.shape[1] // panel
    for d, first in zip(parts, firsts):
        piece = first[...]
        for payload in payloads:
            payload[pl.ds(0, base), pl.ds(d * depth, depth)] = piece
    for i, payload in enumerate(payloads):
        for half in range(2):
            for j in range(chunks):
                at = base + (half * chunks + j) * rows
                block = blocks_ref[pl.ds((2 * i + half) * rows, rows), pl.ds(j * panel, panel)]
                payload[pl.ds(at, rows), :] = block


def plan_body(cubes, grids, slots, owner_hbm, dest_hbm, after_ref, out_ref, owner_ref, dest_ref, slot_ref, count_ref, sems):
    fetches = [
        pltpu.make_async_copy(owner_hbm, owner_ref, sems.at[0]),
        pltpu.make_async_copy(dest_hbm, dest_ref, sems.at[1]),
    ]
    for fetch in fetches:
        fetch.start()
    for fetch in fetches:
        fetch.wait()
    mine = lax.axis_index("cube")
    column = lax.axis_index("grid")
    blocks = owner_ref.shape[0]
    in_range = blocks // grids
    children = dest_ref.shape[0] // cubes
    none = grids * slots
    places = 2 * cubes + grids
    child_places = places + cubes * slots
    for r in range(grids):

        def count_own(i, seen):
            b = r * in_range + i
            own = owner_ref[b] == mine
            slot_ref[b] = jnp.where(own, r * slots + seen, none)
            return seen + own.astype(I32)

        out_ref[2 * cubes + r] = lax.fori_loop(0, in_range, count_own, I32(0), unroll=8)
    for d in range(cubes):
        source = jnp.bitwise_xor(mine, d)
        slot, which = I32(none), I32(0)
        for k in range(children):
            b = dest_ref[source * children + k]
            here = slot_ref[b]
            which = jnp.where(here < none, k, which)
            slot = jnp.minimum(slot, here)
            local_b = b - column * in_range
            inside = jnp.logical_and(local_b >= 0, local_b < in_range)
            out_ref[child_places + d * children + k] = jnp.where(inside, local_b, in_range)
        out_ref[d] = slot
        out_ref[cubes + d] = which
        count_ref[d] = 0
        for k in range(slots):
            out_ref[places + d * slots + k] = in_range

    def place(i, carry):
        d = jnp.bitwise_xor(owner_ref[column * in_range + i], mine)
        k = count_ref[d]
        out_ref[places + d * slots + k] = i
        count_ref[d] = k + 1
        return carry

    lax.fori_loop(0, in_range, place, 0, unroll=8)


def own_body(cubes, grids, span, rows, plan_ref, turned_ref, mine_ref, *refs):
    rests = refs[:grids]
    entries_ref, factor_ref = refs[grids:]
    column = lax.axis_index("grid")
    depth = rests[0].shape[1]
    for e in range(grids):
        r = jnp.bitwise_xor(column, e)
        ids = lax.broadcasted_iota(I32, (span, depth), 0)
        live = ids < plan_ref[2 * cubes + r] * rows
        for d in range(grids):
            if e == 0:
                piece = mine_ref[pl.ds(0, span), pl.ds(d * depth, depth)]
            else:
                k = d ^ e
                at = (k if k < d else k - 1) * span
                piece = rests[d][pl.ds(at, span), :]
            piece = jnp.where(live, piece.astype(F32), 0.0).astype(BF16)
            entries_ref[rows_at(r, span), pl.ds(d * depth, depth)] = piece
    own = jnp.dot(entries_ref[...], turned_ref[...], preferred_element_type=F32)
    factor_ref[pl.ds(0, entries_ref.shape[0]), :] = own.astype(BF16)


def marker_body(after_ref, out_ref):
    out_ref[...] = jnp.zeros_like(out_ref)


def join_body(*refs):
    pass


def add_children(cubes, grids, slots, rows, children, plan_ref, pieces, ranged, touched, total):
    span = slots * rows
    base = span + children * rows
    panel = ranged.shape[1]
    chunks = total.shape[1] // panel
    child_places = 2 * cubes + grids + cubes * slots
    in_range = ranged.shape[0] // rows - 1
    for d, piece in pieces.items():
        at = rows_at(plan_ref[d], rows)
        touched[at, :] += piece[rows_at(slots + plan_ref[cubes + d], rows), :].astype(F32)
        for j in range(chunks):
            part = pl.ds(base + ((d & 1) * chunks + j) * rows, rows)
            total[at, pl.ds(j * panel, panel)] += piece[part, :].astype(F32)
        for k in range(children):
            place = plan_ref[child_places + d * children + k]

            @pl.when(place < in_range)
            def _():
                ranged[rows_at(place, rows), :] += piece[pl.ds(span + k * rows, rows), :].astype(F32)


def early_body(cubes, grids, slots, rows, children, plan_ref, entries_ref, *refs):
    pieces = dict(enumerate(refs[:-3]))
    ranged, touched, total = refs[-3:]
    places = 2 * cubes + grids
    none = entries_ref.shape[0] // rows
    ranged[...] = jnp.zeros_like(ranged)
    total[...] = jnp.zeros_like(total)
    for d in range(cubes):
        slot = plan_ref[d]
        touched[rows_at(slot, rows), :] = entries_ref[rows_at(jnp.minimum(slot, none - 1), rows), :].astype(F32)
    for d, piece in pieces.items():
        for k in range(slots):
            at = rows_at(plan_ref[places + d * slots + k], rows)
            ranged[at, :] = piece[pl.ds(k * rows, rows), :].astype(F32)
    add_children(cubes, grids, slots, rows, children, plan_ref, pieces, ranged, touched, total)


def schur_body(cubes, grids, slots, rows, children, plan_ref, turned_ref, *refs):
    pieces = {cubes - 2: refs[0], cubes - 1: refs[1]}
    out_ref, panel_ref, ranged, touched, total, factor_ref, few = refs[6:]
    column = lax.axis_index("grid")
    own_rows, width = out_ref.shape
    depth = panel_ref.shape[0]
    places = 2 * cubes + grids
    in_range = width // rows
    for d, piece in pieces.items():
        for k in range(slots):
            place = plan_ref[places + d * slots + k]

            @pl.when(place < in_range)
            def _():
                ranged[rows_at(place, rows), :] += piece[pl.ds(k * rows, rows), :].astype(F32)

    add_children(cubes, grids, slots, rows, children, plan_ref, pieces, ranged, touched, total)
    for d in range(cubes):
        few[pl.ds(d * rows, rows), :] = touched[rows_at(plan_ref[d], rows), :].astype(BF16)
    redone = jnp.dot(few[...], turned_ref[...], preferred_element_type=F32).astype(BF16)
    for d in range(cubes):
        factor_ref[rows_at(plan_ref[d], rows), :] = redone[d * rows : (d + 1) * rows, :]
    column_factor = jnp.dot(
        ranged[pl.ds(0, width), :].astype(BF16), turned_ref[...], preferred_element_type=F32
    ).astype(BF16)
    product = lax.dot_general(
        factor_ref[pl.ds(0, own_rows), :], column_factor, (((1,), (1,)), ((), ())), preferred_element_type=F32
    )
    out_ref[...] = (total[pl.ds(0, own_rows), :] - product).astype(BF16)
    if depth % 128 == 0:
        cols = pl.ds(pl.multiple_of(column * depth, depth), depth)
        panel_ref[...] = factor_ref[pl.ds(0, own_rows), cols].astype(F32).T.astype(BF16)
    else:
        for r in range(grids):

            @pl.when(column == r)
            def _():
                part = factor_ref[pl.ds(0, own_rows), pl.ds(r * depth, depth)]
                panel_ref[...] = part.astype(F32).T.astype(BF16)


def local(
    child_update, child_panel, panel_entries, panel_inverse, block_owner, child_dest, child_rows
):
    cubes = lax.axis_size("cube")
    grids = lax.axis_size("grid")
    chips = cubes // 2
    children, rows = child_rows.shape
    width = child_update.shape[1]
    depth = child_panel.shape[0]
    panel = panel_inverse.shape[0]
    own_rows = panel_entries.shape[1]
    slots = own_rows // rows // grids
    span = slots * rows
    base = span + children * rows
    sent = base + 2 * rows * (width // panel)
    like = jax.ShapeDtypeStruct
    small = own_rows * width <= 512 * 512
    kept = pltpu.VMEM if small else like

    def in_hbm(x):
        return pltpu.with_memory_space_constraint(x, pltpu.HBM)

    def join(first, *others, cost=0):
        if small:
            first, *others = (
                pltpu.with_memory_space_constraint(x, pltpu.SMEM if x.dtype == I32 else pltpu.VMEM)
                for x in (first, *others)
            )
        return pl.pallas_call(
            join_body,
            out_shape=kept(first.shape, first.dtype),
            in_specs=[ANY] * (1 + len(others)),
            out_specs=ANY,
            input_output_aliases={0: 0},
            cost_estimate=pl.CostEstimate(flops=cost, bytes_accessed=0, transcendentals=0),
        )(first, *others)

    def swap(x, axis, d):
        n = lax.axis_size(axis)
        return lax.ppermute(x, axis, [(i, i ^ d) for i in range(n)])

    rest_rows = (grids - 1) * span
    *firsts, flipped = call(
        functools.partial(first_body, grids, span),
        [kept((base, depth), BF16)] * grids + [kept((own_rows, depth), BF16)],
        [ANY] * 3,
        [
            pltpu.VMEM(child_rows.shape, I32),
            pltpu.VMEM(child_panel.shape[::-1], BF16),
            pltpu.VMEM(panel_entries.shape, BF16),
            pltpu.SemaphoreType.DMA((3,)),
        ],
        2 * rows * rows * children * depth,
        4 * own_rows * depth,
        limit=28,
    )(in_hbm(child_rows), in_hbm(child_panel.T), in_hbm(panel_entries))
    *rests, blocks, turned = call(
        functools.partial(second_body, cubes, grids, span),
        [kept((rest_rows, depth), BF16)] * grids
        + [kept((cubes * rows, width), BF16), kept((panel, panel), BF16)],
        [ANY] * 5 + [VMEM],
        [
            pltpu.SMEM(block_owner.shape, I32),
            pltpu.SMEM(child_dest.shape, I32),
            pltpu.VMEM(child_rows.shape, I32),
            pltpu.VMEM(child_update.shape, BF16),
            pltpu.SemaphoreType.DMA((4 + grids,)),
        ],
        2 * rows * rows * children * width,
        4 * own_rows * depth,
        limit=28,
    )(*(in_hbm(x) for x in (block_owner, child_dest, child_rows, child_update, panel_inverse)), flipped)
    for d in [*range(2, grids), 1]:
        firsts[d] = swap(firsts[d], "grid", d)
    for d in range(3, grids):
        rests[d] = swap(rests[d], "grid", d)
    parts = [*range(2, grids), 0, 1]
    packed = call(
        functools.partial(pack_body, parts, rows, base),
        [kept((sent, panel), BF16)] * chips,
        [VMEM] * (1 + grids),
        [],
        1000,
        2 * chips * sent * panel,
    )(blocks, *(firsts[d] for d in parts))
    arrived_rest = rests[-1]
    rests[2] = swap(join(rests[2], packed[0]), "grid", 2)
    rests[1] = swap(join(rests[1], rests[-1]), "grid", 1)
    arrived = [packed[0]] + [swap(packed[i], "cube", 2 * i) for i in range(1, chips)]
    rests[-1] = join(rests[-1], packed[0], cost=JOIN_COST)
    last = pltpu.with_memory_space_constraint(arrived_rest, pltpu.VMEM) if small else arrived_rest
    plan = call(
        functools.partial(plan_body, cubes, grids, slots),
        [pltpu.SMEM((2 * cubes + grids + cubes * (slots + children),), I32)],
        [ANY] * 3,
        [
            pltpu.SMEM(block_owner.shape, I32),
            pltpu.SMEM(child_dest.shape, I32),
            pltpu.SMEM(block_owner.shape, I32),
            pltpu.SMEM((cubes,), I32),
            pltpu.SemaphoreType.DMA((2,)),
        ],
        100000,
        6000000,
        [SMEM],
    )(in_hbm(block_owner), in_hbm(child_dest), last)[0]
    plan = pltpu.with_memory_space_constraint(plan, pltpu.SMEM)
    entries, before = call(
        functools.partial(own_body, cubes, grids, span, rows),
        [kept((own_rows, panel), BF16), kept((own_rows + rows, panel), BF16)],
        [SMEM] + [VMEM] * (2 + grids),
        [],
        300000000,
        2 * own_rows * panel * panel,
    )(plan, turned, packed[0], *rests)
    arrived[-1] = join(arrived[-1], *rests[1:])
    pieces = []
    for piece in arrived:
        pieces += [piece, swap(piece, "cube", 1)]
    sizes = (cubes, grids, slots, rows, children)
    shapes = [(width + rows, panel), (own_rows + rows, panel), (own_rows + rows, width)]
    early = call(
        functools.partial(early_body, *sizes),
        [kept(shape, F32) for shape in shapes],
        [SMEM] + [VMEM] * (cubes - 1),
        [],
        1000,
        4 * width * panel,
        limit=16 if small else 56,
    )(plan, entries, *pieces[:-2])
    return tuple(
        call(
            functools.partial(schur_body, *sizes),
            [like((own_rows, width), BF16), like((depth, own_rows), BF16)]
            + [kept(shape, F32) for shape in shapes]
            + [kept((own_rows + rows, panel), BF16)],
            [SMEM] + [VMEM] * 7,
            [pltpu.VMEM((cubes * rows, panel), BF16)],
            2 * own_rows * width * panel,
            2 * (own_rows * width + (own_rows + cubes * span) * panel),
            limit=16 if small else 56,
            aliases={4: 2, 5: 3, 6: 4, 7: 5},
        )(plan, turned, *pieces[-2:], *early, before)[:2]
    )


def solution(mesh):
    placed = (
        P("cube", "grid"),
        P("grid", "cube"),
        P("grid", "cube"),
        P(),
        P(),
        P(),
        P("cube", None),
    )
    return jax.shard_map(
        local,
        mesh=mesh,
        in_specs=placed,
        out_specs=(P("cube", "grid"), P("grid", "cube")),
        check_vma=False,
    )
```

profile of v0, /device:TPU:0, one launch (start us, length us, event | category | flops | bytes accessed | tf_op | source)
XLA Modules:
  0.0 28.3 jit_solution(17876645979386708338)
XLA Ops:
  0.6 1.2 %shard_map.86 = (bf16[192,128]{1,0:T(8,128)(2,1)S(1)}, bf16[192,128]{1,0:T(8,128)(2,1)S(1)}, bf16[192,128]{1,0:T(8,128)(2,1)S(1)}, bf16[192,128]{1,0:T(8,128)(2,1)S(1)}, bf16[512,128]{1,0:T(8,128)(2,1)S(1)}) custom-call(s32[4,16]{1,0:T(4,128)} %rows_hbm.3, bf16[64,128]{1,0:T(8,128)(2,1)} %bitcast.1, bf16[128,512]{1,0:T(8,128)(2,1)} %entries_hbm.1), custom_call_target="tpu_custom_call" | custom-call | flops 262144 | bytes 262144 | tf_op jit(solution)/shard_map/pallas_call | solution.py:331
  1.8 4.1 %collective-permute-start.1 = (bf16[192,128]{1,0:T(8,128)(2,1)S(1)}, bf16[192,128]{1,0:T(8,128)(2,1)S(1)}, u32[]{:S(2)}, u32[]{:S(2)}) collective-permute-start(bf16[192,128]{1,0:T(8,128)(2,1)S(1)} %get-tuple-element.28), channel_id=1, source_target_pairs={{0,2},{1,3},{2,0},{3,1},{4,6},{5,7},{6,4},{7,5},{8,10},{9,11},{10,... | collective-permute-start | bytes 147464 | tf_op jit(solution)/shard_map/ppermute | solution.py:328
  5.9 1.4 %collective-permute-start.2 = (bf16[192,128]{1,0:T(8,128)(2,1)S(1)}, bf16[192,128]{1,0:T(8,128)(2,1)S(1)}, u32[]{:S(2)}, u32[]{:S(2)}) collective-permute-start(bf16[192,128]{1,0:T(8,128)(2,1)S(1)} %get-tuple-element.29), channel_id=1, source_target_pairs={{0,3},{1,2},{2,1},{3,0},{4,7},{5,6},{6,5},{7,4},{8,11},{9,10},{10,... | collective-permute-start | bytes 147464 | tf_op jit(solution)/shard_map/ppermute | solution.py:328
  7.3 0.2 collective-permute-start.3
  7.5 1.2 %shard_map.87 = (bf16[384,128]{1,0:T(8,128)(2,1)S(1)}, bf16[384,128]{1,0:T(8,128)(2,1)S(1)}, bf16[384,128]{1,0:T(8,128)(2,1)S(1)}, bf16[384,128]{1,0:T(8,128)(2,...) custom-call(s32[128]{0:T(128)} %owner_hbm.3, s32[32]{0:T(128)} %dest_hbm.3, s32[4,16]{1,0:T(4,128)} %rows_hbm.3, ...), custom_call_target="tpu_custom_call" | custom-call | flops 1048576 | bytes 262144 | tf_op jit(solution)/shard_map/pallas_call | solution.py:345
  8.7 3.0 %collective-permute-start = (bf16[384,128]{1,0:T(8,128)(2,1)S(1)}, bf16[384,128]{1,0:T(8,128)(2,1)S(1)}, u32[]{:S(2)}, u32[]{:S(2)}) collective-permute-start(bf16[384,128]{1,0:T(8,128)(2,1)S(1)} %get-tuple-element.25), channel_id=1, source_target_pairs={{0,3},{1,2},{2,1},{3,0},{4,7},{5,6},{6,5},{7,4},{8,11},{9,10},{10,... | collective-permute-start | bytes 294920 | tf_op jit(solution)/shard_map/ppermute | solution.py:328
  11.7 0.0 collective-permute-done.1.refs_0_
  11.7 0.2 collective-permute-done.2.refs_1_
  11.9 0.0 collective-permute-done.3.refs_3_
  11.9 0.1 shard_map.89
  12.1 1.6 %collective-permute-start.9 = (bf16[224,512]{1,0:T(8,128)(2,1)S(1)}, bf16[224,512]{1,0:T(8,128)(2,1)S(1)}, u32[]{:S(2)}, u32[]{:S(2)}) collective-permute-start(bf16[224,512]{1,0:T(8,128)(2,1)S(1)} %get-tuple-element.38), channel_id=1, source_target_pairs={{0,8},{4,12},{8,0},{12,4},{16,24},{20,28},{24,16},{28,20},{1,9},{5... | collective-permute-start | bytes 688136 | tf_op jit(solution)/shard_map/ppermute | solution.py:328
  13.6 1.5 %collective-permute-start.11 = (bf16[224,512]{1,0:T(8,128)(2,1)S(1)}, bf16[224,512]{1,0:T(8,128)(2,1)S(1)}, u32[]{:S(2)}, u32[]{:S(2)}) collective-permute-start(bf16[224,512]{1,0:T(8,128)(2,1)S(1)} %get-tuple-element.39), channel_id=1, source_target_pairs={{0,16},{4,20},{8,24},{12,28},{16,0},{20,4},{24,8},{28,12},{1,17},{... | collective-permute-start | bytes 688136 | tf_op jit(solution)/shard_map/ppermute | solution.py:328
  15.1 0.5 %collective-permute-start.4 = (bf16[224,512]{1,0:T(8,128)(2,1)S(1)}, bf16[224,512]{1,0:T(8,128)(2,1)S(1)}, u32[]{:S(2)}, u32[]{:S(2)}) collective-permute-start(bf16[224,512]{1,0:T(8,128)(2,1)S(1)} %get-tuple-element.32), channel_id=1, source_target_pairs={{0,24},{4,28},{8,16},{12,20},{16,8},{20,12},{24,0},{28,4},{1,25},{... | collective-permute-start | bytes 688136 | tf_op jit(solution)/shard_map/ppermute | solution.py:328
  15.6 1.8 %collective-permute-start.6 = (bf16[384,128]{1,0:T(8,128)(2,1)S(1)}, bf16[384,128]{1,0:T(8,128)(2,1)S(1)}, u32[]{:S(2)}, u32[]{:S(2)}) collective-permute-start(bf16[384,128]{1,0:T(8,128)(2,1)S(1)} %shard_map.91), channel_id=1, source_target_pairs={{0,2},{1,3},{2,0},{3,1},{4,6},{5,7},{6,4},{7,5},{8,10},{9,11},{10,... | collective-permute-start | bytes 294920 | tf_op jit(solution)/shard_map/ppermute | solution.py:328
  17.4 1.1 %collective-permute-start.5 = (bf16[384,128]{1,0:T(8,128)(2,1)S(1)}, bf16[384,128]{1,0:T(8,128)(2,1)S(1)}, u32[]{:S(2)}, u32[]{:S(2)}) collective-permute-start(bf16[384,128]{1,0:T(8,128)(2,1)S(1)} %shard_map.90), channel_id=1, source_target_pairs={{0,1},{1,0},{2,3},{3,2},{4,5},{5,4},{6,7},{7,6},{8,9},{9,8},{10,11... | collective-permute-start | bytes 294920 | tf_op jit(solution)/shard_map/ppermute | solution.py:328
  18.5 1.4 %shard_map.88.plan_ref = s32[116]{0:T(128)S(4)} custom-call(s32[128]{0:T(128)} %owner_hbm.3, s32[32]{0:T(128)} %dest_hbm.3, bf16[384,128]{1,0:T(8,128)(2,1)S(1)} %collective-permute-done.after_ref.refs_1_.refs_0_), custom_call_target="tpu_custom_call" | custom-call | flops 100000 | bytes 6000000 | tf_op jit(solution)/shard_map/pallas_call | solution.py:380
  19.9 2.1 %collective-permute-done.6.refs_2_ = bf16[384,128]{1,0:T(8,128)(2,1)S(1)} collective-permute-done((bf16[384,128]{1,0:T(8,128)(2,1)S(1)}, bf16[384,128]{1,0:T(8,128)(2,1)S(1)}, u32[]{:S(2)}, u32[]{:S(2)}) %collective-permute-start.6) | collective-permute-done | bytes 98336 | tf_op jit(solution)/shard_map/ppermute | solution.py:328
  22.0 0.5 %collective-permute-start.10 = (bf16[224,512]{1,0:T(8,128)(2,1)S(1)}, bf16[224,512]{1,0:T(8,128)(2,1)S(1)}, u32[]{:S(2)}, u32[]{:S(2)}) collective-permute-start(bf16[224,512]{1,0:T(8,128)(2,1)S(1)} %collective-permute-done.9.refs_2_), channel_id=1, source_target_pairs={{0,4},{4,0},{8,12},{12,8},{16,20},{20,16},{24,28},{28,24},{1,5},{5... | collective-permute-start | bytes 688136 | tf_op jit(solution)/shard_map/ppermute | solution.py:328
  22.5 1.8 %collective-permute-done.11.refs_4_ = bf16[224,512]{1,0:T(8,128)(2,1)S(1)} collective-permute-done((bf16[224,512]{1,0:T(8,128)(2,1)S(1)}, bf16[224,512]{1,0:T(8,128)(2,1)S(1)}, u32[]{:S(2)}, u32[]{:S(2)}) %collective-permute-start.11) | collective-permute-done | bytes 229408 | tf_op jit(solution)/shard_map/ppermute | solution.py:328
  24.3 0.5 %collective-permute-start.7 = (bf16[224,512]{1,0:T(8,128)(2,1)S(1)}, bf16[224,512]{1,0:T(8,128)(2,1)S(1)}, u32[]{:S(2)}, u32[]{:S(2)}) collective-permute-start(bf16[224,512]{1,0:T(8,128)(2,1)S(1)} %shard_map.93.refs_0_), channel_id=1, source_target_pairs={{0,4},{4,0},{8,12},{12,8},{16,20},{20,16},{24,28},{28,24},{1,5},{5... | collective-permute-start | bytes 688136 | tf_op jit(solution)/shard_map/ppermute | solution.py:328
  24.8 0.5 %shard_map.94 = (bf16[512,512]{1,0:T(8,128)(2,1)S(1)}, bf16[528,512]{1,0:T(8,128)(2,1)S(1)}) custom-call(s32[116]{0:T(128)S(4)} %shard_map.88.plan_ref, bf16[512,512]{1,0:T(8,128)(2,1)S(1)} %get-tuple-element.26.turned_ref, bf16[224,512]{1,0:T(8,128)(2,1)S(1)} %get-tuple-element.35.refs_1_.mine_ref.refs_0_, bf16[384,128]{1,0:T(8,128)(2,1)S(1)} %get-tuple-element.36.refs_0_, ...), custom_call_target="tpu_custom_call" | custom-call | flops 300000000 | bytes 268435456 | tf_op jit(solution)/shard_map/pallas_call | solution.py:396
  25.4 0.4 %collective-permute-done.12.refs_5_ = bf16[224,512]{1,0:T(8,128)(2,1)S(1)} collective-permute-done((bf16[224,512]{1,0:T(8,128)(2,1)S(1)}, bf16[224,512]{1,0:T(8,128)(2,1)S(1)}, u32[]{:S(2)}, u32[]{:S(2)}) %collective-permute-start.12) | collective-permute-done | bytes 229408 | tf_op jit(solution)/shard_map/ppermute | solution.py:328
  25.8 0.5 %shard_map.95 = (f32[528,512]{1,0:T(8,128)S(1)}, f32[528,512]{1,0:T(8,128)S(1)}, f32[528,512]{1,0:T(8,128)S(1)}) custom-call(s32[116]{0:T(128)S(4)} %shard_map.88.plan_ref, bf16[512,512]{1,0:T(8,128)(2,1)S(1)} %get-tuple-element.37.entries_ref, bf16[224,512]{1,0:T(8,128)(2,1)S(1)} %get-tuple-element.35.refs_1_.mine_ref.refs_0_, ...), custom_call_target="tpu_custom_call" | custom-call | flops 1000 | bytes 1048576 | tf_op jit(solution)/shard_map/pallas_call | solution.py:410
  26.3 1.9 %shard_map.96 = (bf16[512,512]{1,0:T(8,128)(2,1)}, bf16[128,512]{1,0:T(8,128)(2,1)}, f32[528,512]{1,0:T(8,128)S(1)}, f32[528,512]{1,0:T(8,128)S(1)}, f32[528,512...) custom-call(s32[116]{0:T(128)S(4)} %shard_map.88.plan_ref, ...), custom_call_target="tpu_custom_call", output_to_operand_aliasing={{2}: (4, {}), {3}: (5, {}), {4}: (6, {}), {5}: (7, {})} | custom-call | flops 268435456 | bytes 2097152 | tf_op jit(solution)/shard_map/pallas_call | solution.py:420
  (13 shorter events, 0.0 us)
Async XLA Ops:
  1.8 9.9 %collective-permute-start.1 = (bf16[192,128]{1,0:T(8,128)(2,1)S(1)}, bf16[192,128]{1,0:T(8,128)(2,1)S(1)}, u32[]{:S(2)}, u32[]{:S(2)}) collective-permute-start(bf16[192,128]{1,0:T(8,128)(2,1)S(1)} %get-tuple-element.28), channel_id=1, source_target_pairs={{0,2},{1,3},{2,0},{3,1},{4,6},{5,7},{6,4},{7,5},{8,10},{9,11},{10,... | collective-permute-start | bytes 147464 | tf_op jit(solution)/shard_map/ppermute | solution.py:328
  5.9 6.0 %collective-permute-start.2 = (bf16[192,128]{1,0:T(8,128)(2,1)S(1)}, bf16[192,128]{1,0:T(8,128)(2,1)S(1)}, u32[]{:S(2)}, u32[]{:S(2)}) collective-permute-start(bf16[192,128]{1,0:T(8,128)(2,1)S(1)} %get-tuple-element.29), channel_id=1, source_target_pairs={{0,3},{1,2},{2,1},{3,0},{4,7},{5,6},{6,5},{7,4},{8,11},{9,10},{10,... | collective-permute-start | bytes 147464 | tf_op jit(solution)/shard_map/ppermute | solution.py:328
  7.3 4.6 %collective-permute-start.3 = (bf16[192,128]{1,0:T(8,128)(2,1)S(1)}, bf16[192,128]{1,0:T(8,128)(2,1)S(1)}, u32[]{:S(2)}, u32[]{:S(2)}) collective-permute-start(bf16[192,128]{1,0:T(8,128)(2,1)S(1)} %get-tuple-element.31), channel_id=1, source_target_pairs={{0,1},{1,0},{2,3},{3,2},{4,5},{5,4},{6,7},{7,6},{8,9},{9,8},{10,11... | collective-permute-start | bytes 147464 | tf_op jit(solution)/shard_map/ppermute | solution.py:328
  8.7 8.6 %collective-permute-start = (bf16[384,128]{1,0:T(8,128)(2,1)S(1)}, bf16[384,128]{1,0:T(8,128)(2,1)S(1)}, u32[]{:S(2)}, u32[]{:S(2)}) collective-permute-start(bf16[384,128]{1,0:T(8,128)(2,1)S(1)} %get-tuple-element.25), channel_id=1, source_target_pairs={{0,3},{1,2},{2,1},{3,0},{4,7},{5,6},{6,5},{7,4},{8,11},{9,10},{10,... | collective-permute-start | bytes 294920 | tf_op jit(solution)/shard_map/ppermute | solution.py:328
  12.1 9.9 %collective-permute-start.9 = (bf16[224,512]{1,0:T(8,128)(2,1)S(1)}, bf16[224,512]{1,0:T(8,128)(2,1)S(1)}, u32[]{:S(2)}, u32[]{:S(2)}) collective-permute-start(bf16[224,512]{1,0:T(8,128)(2,1)S(1)} %get-tuple-element.38), channel_id=1, source_target_pairs={{0,8},{4,12},{8,0},{12,4},{16,24},{20,28},{24,16},{28,20},{1,9},{5... | collective-permute-start | bytes 688136 | tf_op jit(solution)/shard_map/ppermute | solution.py:328
  13.6 10.7 %collective-permute-start.11 = (bf16[224,512]{1,0:T(8,128)(2,1)S(1)}, bf16[224,512]{1,0:T(8,128)(2,1)S(1)}, u32[]{:S(2)}, u32[]{:S(2)}) collective-permute-start(bf16[224,512]{1,0:T(8,128)(2,1)S(1)} %get-tuple-element.39), channel_id=1, source_target_pairs={{0,16},{4,20},{8,24},{12,28},{16,0},{20,4},{24,8},{28,12},{1,17},{... | collective-permute-start | bytes 688136 | tf_op jit(solution)/shard_map/ppermute | solution.py:328
  15.1 9.2 %collective-permute-start.4 = (bf16[224,512]{1,0:T(8,128)(2,1)S(1)}, bf16[224,512]{1,0:T(8,128)(2,1)S(1)}, u32[]{:S(2)}, u32[]{:S(2)}) collective-permute-start(bf16[224,512]{1,0:T(8,128)(2,1)S(1)} %get-tuple-element.32), channel_id=1, source_target_pairs={{0,24},{4,28},{8,16},{12,20},{16,8},{20,12},{24,0},{28,4},{1,25},{... | collective-permute-start | bytes 688136 | tf_op jit(solution)/shard_map/ppermute | solution.py:328
  15.6 6.4 %collective-permute-start.6 = (bf16[384,128]{1,0:T(8,128)(2,1)S(1)}, bf16[384,128]{1,0:T(8,128)(2,1)S(1)}, u32[]{:S(2)}, u32[]{:S(2)}) collective-permute-start(bf16[384,128]{1,0:T(8,128)(2,1)S(1)} %shard_map.91), channel_id=1, source_target_pairs={{0,2},{1,3},{2,0},{3,1},{4,6},{5,7},{6,4},{7,5},{8,10},{9,11},{10,... | collective-permute-start | bytes 294920 | tf_op jit(solution)/shard_map/ppermute | solution.py:328
  17.4 6.9 %collective-permute-start.5 = (bf16[384,128]{1,0:T(8,128)(2,1)S(1)}, bf16[384,128]{1,0:T(8,128)(2,1)S(1)}, u32[]{:S(2)}, u32[]{:S(2)}) collective-permute-start(bf16[384,128]{1,0:T(8,128)(2,1)S(1)} %shard_map.90), channel_id=1, source_target_pairs={{0,1},{1,0},{2,3},{3,2},{4,5},{5,4},{6,7},{7,6},{8,9},{9,8},{10,11... | collective-permute-start | bytes 294920 | tf_op jit(solution)/shard_map/ppermute | solution.py:328
  22.0 3.4 %collective-permute-start.8 = (bf16[224,512]{1,0:T(8,128)(2,1)S(1)}, bf16[224,512]{1,0:T(8,128)(2,1)S(1)}, u32[]{:S(2)}, u32[]{:S(2)}) collective-permute-start(bf16[224,512]{1,0:T(8,128)(2,1)S(1)} %get-tuple-element.35.refs_1_.mine_ref.refs_0_), channel_id=1, source_target_pairs={{0,4},{4,0},{8,12},{12,8},{16,20},{20,16},{24,28},{28,24},{1,5},{5... | collective-permute-start | bytes 688136 | tf_op jit(solution)/shard_map/ppermute | solution.py:328
  22.0 3.4 %collective-permute-start.10 = (bf16[224,512]{1,0:T(8,128)(2,1)S(1)}, bf16[224,512]{1,0:T(8,128)(2,1)S(1)}, u32[]{:S(2)}, u32[]{:S(2)}) collective-permute-start(bf16[224,512]{1,0:T(8,128)(2,1)S(1)} %collective-permute-done.9.refs_2_), channel_id=1, source_target_pairs={{0,4},{4,0},{8,12},{12,8},{16,20},{20,16},{24,28},{28,24},{1,5},{5... | collective-permute-start | bytes 688136 | tf_op jit(solution)/shard_map/ppermute | solution.py:328
  24.3 1.5 %collective-permute-start.12 = (bf16[224,512]{1,0:T(8,128)(2,1)S(1)}, bf16[224,512]{1,0:T(8,128)(2,1)S(1)}, u32[]{:S(2)}, u32[]{:S(2)}) collective-permute-start(bf16[224,512]{1,0:T(8,128)(2,1)S(1)} %collective-permute-done.11.refs_4_), channel_id=1, source_target_pairs={{0,4},{4,0},{8,12},{12,8},{16,20},{20,16},{24,28},{28,24},{1,5},{5... | collective-permute-start | bytes 688136 | tf_op jit(solution)/shard_map/ppermute | solution.py:328
  24.3 2.0 %collective-permute-start.7 = (bf16[224,512]{1,0:T(8,128)(2,1)S(1)}, bf16[224,512]{1,0:T(8,128)(2,1)S(1)}, u32[]{:S(2)}, u32[]{:S(2)}) collective-permute-start(bf16[224,512]{1,0:T(8,128)(2,1)S(1)} %shard_map.93.refs_0_), channel_id=1, source_target_pairs={{0,4},{4,0},{8,12},{12,8},{16,20},{20,16},{24,28},{28,24},{1,5},{5... | collective-permute-start | bytes 688136 | tf_op jit(solution)/shard_map/ppermute | solution.py:328
where the time goes:
time: 28.4 us; the launch traced here: 28.3 us
  starting transfers between devices  16.1 us (57%)
  Pallas kernels  6.98 us (25%)
  waiting for transfers between devices  4.45 us (16%)
  between operations  0.73 us (3%)
    ppermute x13, starting transfers between devices, swap(): return lax.ppermute(x, axis, [(i, i ^ d) for i in range(n)])  16.1 us
    ppermute x13, waiting for transfers between devices, swap(): return lax.ppermute(x, axis, [(i, i ^ d) for i in range(n)])  4.45 us
    pallas_call x1, Pallas kernels, local(): call(functools.partial(schur_body, *sizes), [like((own_rows, width), BF16...  1.95 us
    pallas_call x1, Pallas kernels, local(): call(functools.partial(plan_body, cubes, grids, slots), [pltpu.SMEM((2 *...  1.42 us
    pallas_call x1, Pallas kernels, local(): call(functools.partial(second_body, cubes, grids, span), [kept((rest_rows...  1.22 us
    pallas_call x1, Pallas kernels, local(): call(functools.partial(first_body, grids, span), [kept((base, depth), BF1...  1.2 us
  transfers between devices with their start and end apart: 13, of which 4 were waited for; matrix products, arithmetic and copies ran while one was open for 0% of the time, Pallas kernels for 14%

commit v1 on v0

--- a/solution.py
+++ b/solution.py
@@ -362,7 +362,7 @@
         firsts[d] = swap(firsts[d], "grid", d)
     for d in range(3, grids):
         rests[d] = swap(rests[d], "grid", d)
-    parts = [*range(2, grids), 0, 1]
+    parts = [*range(grids - 1, 1, -1), 0, 1]
     packed = call(
         functools.partial(pack_body, parts, rows, base),
         [kept((sent, panel), BF16)] * chips,

time: 28.4 us -> 29.3 us (1.032)
  waiting for transfers between devices: 4.45 us -> 5.32 us
    ppermute x13, waiting for transfers between devices: 4.45 us -> 5.32 us  [swap(): return lax.ppermute(x, axis, [(i, i ^ d) for i in range(n)])]
  transfers between devices with their start and end apart: 13 -> 13, of which waited for: 4 -> 3; matrix products, arithmetic and copies ran while one was open for 0% -> 0% of each run, Pallas kernels for 14% -> 13%
where the time goes in v1:
time: 29.3 us; the launch traced here: 29.2 us
  starting transfers between devices  16.1 us (55%)
  Pallas kernels  6.99 us (24%)
  waiting for transfers between devices  5.32 us (18%)
  between operations  0.73 us (2%)
    ppermute x13, starting transfers between devices, swap(): return lax.ppermute(x, axis, [(i, i ^ d) for i in range(n)])  16.1 us
    ppermute x13, waiting for transfers between devices, swap(): return lax.ppermute(x, axis, [(i, i ^ d) for i in range(n)])  5.32 us
    pallas_call x1, Pallas kernels, local(): call(functools.partial(schur_body, *sizes), [like((own_rows, width), BF16...  1.96 us
    pallas_call x1, Pallas kernels, local(): call(functools.partial(plan_body, cubes, grids, slots), [pltpu.SMEM((2 *...  1.42 us
    pallas_call x1, Pallas kernels, local(): call(functools.partial(second_body, cubes, grids, span), [kept((rest_rows...  1.22 us
    pallas_call x1, Pallas kernels, local(): call(functools.partial(first_body, grids, span), [kept((base, depth), BF1...  1.2 us
  transfers between devices with their start and end apart: 13, of which 3 were waited for; matrix products, arithmetic and copies ran while one was open for 0% of the time, Pallas kernels for 13%

profile of v1, /device:TPU:0, one launch (start us, length us, event | category | flops | bytes accessed | tf_op | source)
XLA Modules:
  0.0 29.2 jit_solution(5979533915580834769)
XLA Ops:
  0.6 1.2 %shard_map.86 = (bf16[192,128]{1,0:T(8,128)(2,1)S(1)}, bf16[192,128]{1,0:T(8,128)(2,1)S(1)}, bf16[192,128]{1,0:T(8,128)(2,1)S(1)}, bf16[192,128]{1,0:T(8,128)(2,1)S(1)}, bf16[512,128]{1,0:T(8,128)(2,1)S(1)}) custom-call(s32[4,16]{1,0:T(4,128)} %rows_hbm.3, bf16[64,128]{1,0:T(8,128)(2,1)} %bitcast.1, bf16[128,512]{1,0:T(8,128)(2,1)} %entries_hbm.1), custom_call_target="tpu_custom_call" | custom-call | flops 262144 | bytes 262144 | tf_op jit(solution)/shard_map/pallas_call | solution.py:331
  1.8 5.1 %collective-permute-start.1 = (bf16[192,128]{1,0:T(8,128)(2,1)S(1)}, bf16[192,128]{1,0:T(8,128)(2,1)S(1)}, u32[]{:S(2)}, u32[]{:S(2)}) collective-permute-start(bf16[192,128]{1,0:T(8,128)(2,1)S(1)} %get-tuple-element.28), channel_id=1, source_target_pairs={{0,3},{1,2},{2,1},{3,0},{4,7},{5,6},{6,5},{7,4},{8,11},{9,10},{10,... | collective-permute-start | bytes 147464 | tf_op jit(solution)/shard_map/ppermute | solution.py:328
  6.9 0.0 collective-permute-start.2
  6.9 0.6 %collective-permute-start.3 = (bf16[192,128]{1,0:T(8,128)(2,1)S(1)}, bf16[192,128]{1,0:T(8,128)(2,1)S(1)}, u32[]{:S(2)}, u32[]{:S(2)}) collective-permute-start(bf16[192,128]{1,0:T(8,128)(2,1)S(1)} %get-tuple-element.31), channel_id=1, source_target_pairs={{0,1},{1,0},{2,3},{3,2},{4,5},{5,4},{6,7},{7,6},{8,9},{9,8},{10,11... | collective-permute-start | bytes 147464 | tf_op jit(solution)/shard_map/ppermute | solution.py:328
  7.6 1.2 %shard_map.87 = (bf16[384,128]{1,0:T(8,128)(2,1)S(1)}, bf16[384,128]{1,0:T(8,128)(2,1)S(1)}, bf16[384,128]{1,0:T(8,128)(2,1)S(1)}, bf16[384,128]{1,0:T(8,128)(2,...) custom-call(s32[128]{0:T(128)} %owner_hbm.3, s32[32]{0:T(128)} %dest_hbm.3, s32[4,16]{1,0:T(4,128)} %rows_hbm.3, ...), custom_call_target="tpu_custom_call" | custom-call | flops 1048576 | bytes 262144 | tf_op jit(solution)/shard_map/pallas_call | solution.py:345
  8.8 3.8 %collective-permute-start = (bf16[384,128]{1,0:T(8,128)(2,1)S(1)}, bf16[384,128]{1,0:T(8,128)(2,1)S(1)}, u32[]{:S(2)}, u32[]{:S(2)}) collective-permute-start(bf16[384,128]{1,0:T(8,128)(2,1)S(1)} %get-tuple-element.25), channel_id=1, source_target_pairs={{0,3},{1,2},{2,1},{3,0},{4,7},{5,6},{6,5},{7,4},{8,11},{9,10},{10,... | collective-permute-start | bytes 294920 | tf_op jit(solution)/shard_map/ppermute | solution.py:328
  12.6 0.1 shard_map.89
  12.8 1.6 %collective-permute-start.9 = (bf16[224,512]{1,0:T(8,128)(2,1)S(1)}, bf16[224,512]{1,0:T(8,128)(2,1)S(1)}, u32[]{:S(2)}, u32[]{:S(2)}) collective-permute-start(bf16[224,512]{1,0:T(8,128)(2,1)S(1)} %get-tuple-element.38), channel_id=1, source_target_pairs={{0,8},{4,12},{8,0},{12,4},{16,24},{20,28},{24,16},{28,20},{1,9},{5... | collective-permute-start | bytes 688136 | tf_op jit(solution)/shard_map/ppermute | solution.py:328
  14.3 1.5 %collective-permute-start.11 = (bf16[224,512]{1,0:T(8,128)(2,1)S(1)}, bf16[224,512]{1,0:T(8,128)(2,1)S(1)}, u32[]{:S(2)}, u32[]{:S(2)}) collective-permute-start(bf16[224,512]{1,0:T(8,128)(2,1)S(1)} %get-tuple-element.39), channel_id=1, source_target_pairs={{0,16},{4,20},{8,24},{12,28},{16,0},{20,4},{24,8},{28,12},{1,17},{... | collective-permute-start | bytes 688136 | tf_op jit(solution)/shard_map/ppermute | solution.py:328
  15.9 0.5 %collective-permute-start.4 = (bf16[224,512]{1,0:T(8,128)(2,1)S(1)}, bf16[224,512]{1,0:T(8,128)(2,1)S(1)}, u32[]{:S(2)}, u32[]{:S(2)}) collective-permute-start(bf16[224,512]{1,0:T(8,128)(2,1)S(1)} %get-tuple-element.32), channel_id=1, source_target_pairs={{0,24},{4,28},{8,16},{12,20},{16,8},{20,12},{24,0},{28,4},{1,25},{... | collective-permute-start | bytes 688136 | tf_op jit(solution)/shard_map/ppermute | solution.py:328
  16.3 1.8 %collective-permute-start.6 = (bf16[384,128]{1,0:T(8,128)(2,1)S(1)}, bf16[384,128]{1,0:T(8,128)(2,1)S(1)}, u32[]{:S(2)}, u32[]{:S(2)}) collective-permute-start(bf16[384,128]{1,0:T(8,128)(2,1)S(1)} %shard_map.91), channel_id=1, source_target_pairs={{0,2},{1,3},{2,0},{3,1},{4,6},{5,7},{6,4},{7,5},{8,10},{9,11},{10,... | collective-permute-start | bytes 294920 | tf_op jit(solution)/shard_map/ppermute | solution.py:328
  18.2 0.0 collective-permute-done.after_ref.refs_1_.refs_0_
  18.2 0.2 collective-permute-start.5
  18.3 1.4 %shard_map.88.plan_ref = s32[116]{0:T(128)S(4)} custom-call(s32[128]{0:T(128)} %owner_hbm.3, s32[32]{0:T(128)} %dest_hbm.3, bf16[384,128]{1,0:T(8,128)(2,1)S(1)} %collective-permute-done.after_ref.refs_1_.refs_0_), custom_call_target="tpu_custom_call" | custom-call | flops 100000 | bytes 6000000 | tf_op jit(solution)/shard_map/pallas_call | solution.py:380
  19.8 2.5 %collective-permute-done.6.refs_2_ = bf16[384,128]{1,0:T(8,128)(2,1)S(1)} collective-permute-done((bf16[384,128]{1,0:T(8,128)(2,1)S(1)}, bf16[384,128]{1,0:T(8,128)(2,1)S(1)}, u32[]{:S(2)}, u32[]{:S(2)}) %collective-permute-start.6) | collective-permute-done | bytes 98336 | tf_op jit(solution)/shard_map/ppermute | solution.py:328
  22.3 0.5 %collective-permute-start.10 = (bf16[224,512]{1,0:T(8,128)(2,1)S(1)}, bf16[224,512]{1,0:T(8,128)(2,1)S(1)}, u32[]{:S(2)}, u32[]{:S(2)}) collective-permute-start(bf16[224,512]{1,0:T(8,128)(2,1)S(1)} %collective-permute-done.9.refs_2_), channel_id=1, source_target_pairs={{0,4},{4,0},{8,12},{12,8},{16,20},{20,16},{24,28},{28,24},{1,5},{5... | collective-permute-start | bytes 688136 | tf_op jit(solution)/shard_map/ppermute | solution.py:328
  22.9 2.3 %collective-permute-done.11.refs_4_ = bf16[224,512]{1,0:T(8,128)(2,1)S(1)} collective-permute-done((bf16[224,512]{1,0:T(8,128)(2,1)S(1)}, bf16[224,512]{1,0:T(8,128)(2,1)S(1)}, u32[]{:S(2)}, u32[]{:S(2)}) %collective-permute-start.11) | collective-permute-done | bytes 229408 | tf_op jit(solution)/shard_map/ppermute | solution.py:328
  25.2 0.0 collective-permute-start.12
  25.2 0.5 %collective-permute-start.7 = (bf16[224,512]{1,0:T(8,128)(2,1)S(1)}, bf16[224,512]{1,0:T(8,128)(2,1)S(1)}, u32[]{:S(2)}, u32[]{:S(2)}) collective-permute-start(bf16[224,512]{1,0:T(8,128)(2,1)S(1)} %shard_map.93.refs_0_), channel_id=1, source_target_pairs={{0,4},{4,0},{8,12},{12,8},{16,20},{20,16},{24,28},{28,24},{1,5},{5... | collective-permute-start | bytes 688136 | tf_op jit(solution)/shard_map/ppermute | solution.py:328
  25.7 0.5 %shard_map.94 = (bf16[512,512]{1,0:T(8,128)(2,1)S(1)}, bf16[528,512]{1,0:T(8,128)(2,1)S(1)}) custom-call(s32[116]{0:T(128)S(4)} %shard_map.88.plan_ref, bf16[512,512]{1,0:T(8,128)(2,1)S(1)} %get-tuple-element.26.turned_ref, bf16[224,512]{1,0:T(8,128)(2,1)S(1)} %get-tuple-element.35.refs_1_.mine_ref.refs_0_, bf16[384,128]{1,0:T(8,128)(2,1)S(1)} %get-tuple-element.36.refs_0_, ...), custom_call_target="tpu_custom_call" | custom-call | flops 300000000 | bytes 268435456 | tf_op jit(solution)/shard_map/pallas_call | solution.py:396
  26.3 0.0 collective-permute-done.8.refs_1_
  26.3 0.4 %collective-permute-done.12.refs_5_ = bf16[224,512]{1,0:T(8,128)(2,1)S(1)} collective-permute-done((bf16[224,512]{1,0:T(8,128)(2,1)S(1)}, bf16[224,512]{1,0:T(8,128)(2,1)S(1)}, u32[]{:S(2)}, u32[]{:S(2)}) %collective-permute-start.12) | collective-permute-done | bytes 229408 | tf_op jit(solution)/shard_map/ppermute | solution.py:328
  26.7 0.5 %shard_map.95 = (f32[528,512]{1,0:T(8,128)S(1)}, f32[528,512]{1,0:T(8,128)S(1)}, f32[528,512]{1,0:T(8,128)S(1)}) custom-call(s32[116]{0:T(128)S(4)} %shard_map.88.plan_ref, bf16[512,512]{1,0:T(8,128)(2,1)S(1)} %get-tuple-element.37.entries_ref, bf16[224,512]{1,0:T(8,128)(2,1)S(1)} %get-tuple-element.35.refs_1_.mine_ref.refs_0_, ...), custom_call_target="tpu_custom_call" | custom-call | flops 1000 | bytes 1048576 | tf_op jit(solution)/shard_map/pallas_call | solution.py:410
  27.2 2.0 %shard_map.96 = (bf16[512,512]{1,0:T(8,128)(2,1)}, bf16[128,512]{1,0:T(8,128)(2,1)}, f32[528,512]{1,0:T(8,128)S(1)}, f32[528,512]{1,0:T(8,128)S(1)}, f32[528,512...) custom-call(s32[116]{0:T(128)S(4)} %shard_map.88.plan_ref, ...), custom_call_target="tpu_custom_call", output_to_operand_aliasing={{2}: (4, {}), {3}: (5, {}), {4}: (6, {}), {5}: (7, {})} | custom-call | flops 268435456 | bytes 2097152 | tf_op jit(solution)/shard_map/pallas_call | solution.py:420
  (13 shorter events, 0.0 us)
Async XLA Ops:
  1.8 10.8 %collective-permute-start.1 = (bf16[192,128]{1,0:T(8,128)(2,1)S(1)}, bf16[192,128]{1,0:T(8,128)(2,1)S(1)}, u32[]{:S(2)}, u32[]{:S(2)}) collective-permute-start(bf16[192,128]{1,0:T(8,128)(2,1)S(1)} %get-tuple-element.28), channel_id=1, source_target_pairs={{0,3},{1,2},{2,1},{3,0},{4,7},{5,6},{6,5},{7,4},{8,11},{9,10},{10,... | collective-permute-start | bytes 147464 | tf_op jit(solution)/shard_map/ppermute | solution.py:328
  6.9 5.7 %collective-permute-start.2 = (bf16[192,128]{1,0:T(8,128)(2,1)S(1)}, bf16[192,128]{1,0:T(8,128)(2,1)S(1)}, u32[]{:S(2)}, u32[]{:S(2)}) collective-permute-start(bf16[192,128]{1,0:T(8,128)(2,1)S(1)} %get-tuple-element.29), channel_id=1, source_target_pairs={{0,2},{1,3},{2,0},{3,1},{4,6},{5,7},{6,4},{7,5},{8,10},{9,11},{10,... | collective-permute-start | bytes 147464 | tf_op jit(solution)/shard_map/ppermute | solution.py:328
  6.9 5.7 %collective-permute-start.3 = (bf16[192,128]{1,0:T(8,128)(2,1)S(1)}, bf16[192,128]{1,0:T(8,128)(2,1)S(1)}, u32[]{:S(2)}, u32[]{:S(2)}) collective-permute-start(bf16[192,128]{1,0:T(8,128)(2,1)S(1)} %get-tuple-element.31), channel_id=1, source_target_pairs={{0,1},{1,0},{2,3},{3,2},{4,5},{5,4},{6,7},{7,6},{8,9},{9,8},{10,11... | collective-permute-start | bytes 147464 | tf_op jit(solution)/shard_map/ppermute | solution.py:328
  8.8 9.4 %collective-permute-start = (bf16[384,128]{1,0:T(8,128)(2,1)S(1)}, bf16[384,128]{1,0:T(8,128)(2,1)S(1)}, u32[]{:S(2)}, u32[]{:S(2)}) collective-permute-start(bf16[384,128]{1,0:T(8,128)(2,1)S(1)} %get-tuple-element.25), channel_id=1, source_target_pairs={{0,3},{1,2},{2,1},{3,0},{4,7},{5,6},{6,5},{7,4},{8,11},{9,10},{10,... | collective-permute-start | bytes 294920 | tf_op jit(solution)/shard_map/ppermute | solution.py:328
  12.8 9.6 %collective-permute-start.9 = (bf16[224,512]{1,0:T(8,128)(2,1)S(1)}, bf16[224,512]{1,0:T(8,128)(2,1)S(1)}, u32[]{:S(2)}, u32[]{:S(2)}) collective-permute-start(bf16[224,512]{1,0:T(8,128)(2,1)S(1)} %get-tuple-element.38), channel_id=1, source_target_pairs={{0,8},{4,12},{8,0},{12,4},{16,24},{20,28},{24,16},{28,20},{1,9},{5... | collective-permute-start | bytes 688136 | tf_op jit(solution)/shard_map/ppermute | solution.py:328
  14.3 10.9 %collective-permute-start.11 = (bf16[224,512]{1,0:T(8,128)(2,1)S(1)}, bf16[224,512]{1,0:T(8,128)(2,1)S(1)}, u32[]{:S(2)}, u32[]{:S(2)}) collective-permute-start(bf16[224,512]{1,0:T(8,128)(2,1)S(1)} %get-tuple-element.39), channel_id=1, source_target_pairs={{0,16},{4,20},{8,24},{12,28},{16,0},{20,4},{24,8},{28,12},{1,17},{... | collective-permute-start | bytes 688136 | tf_op jit(solution)/shard_map/ppermute | solution.py:328
  15.9 9.3 %collective-permute-start.4 = (bf16[224,512]{1,0:T(8,128)(2,1)S(1)}, bf16[224,512]{1,0:T(8,128)(2,1)S(1)}, u32[]{:S(2)}, u32[]{:S(2)}) collective-permute-start(bf16[224,512]{1,0:T(8,128)(2,1)S(1)} %get-tuple-element.32), channel_id=1, source_target_pairs={{0,24},{4,28},{8,16},{12,20},{16,8},{20,12},{24,0},{28,4},{1,25},{... | collective-permute-start | bytes 688136 | tf_op jit(solution)/shard_map/ppermute | solution.py:328
  16.3 6.0 %collective-permute-start.6 = (bf16[384,128]{1,0:T(8,128)(2,1)S(1)}, bf16[384,128]{1,0:T(8,128)(2,1)S(1)}, u32[]{:S(2)}, u32[]{:S(2)}) collective-permute-start(bf16[384,128]{1,0:T(8,128)(2,1)S(1)} %shard_map.91), channel_id=1, source_target_pairs={{0,2},{1,3},{2,0},{3,1},{4,6},{5,7},{6,4},{7,5},{8,10},{9,11},{10,... | collective-permute-start | bytes 294920 | tf_op jit(solution)/shard_map/ppermute | solution.py:328
  18.2 7.0 %collective-permute-start.5 = (bf16[384,128]{1,0:T(8,128)(2,1)S(1)}, bf16[384,128]{1,0:T(8,128)(2,1)S(1)}, u32[]{:S(2)}, u32[]{:S(2)}) collective-permute-start(bf16[384,128]{1,0:T(8,128)(2,1)S(1)} %shard_map.90), channel_id=1, source_target_pairs={{0,1},{1,0},{2,3},{3,2},{4,5},{5,4},{6,7},{7,6},{8,9},{9,8},{10,11... | collective-permute-start | bytes 294920 | tf_op jit(solution)/shard_map/ppermute | solution.py:328
  22.3 3.9 %collective-permute-start.8 = (bf16[224,512]{1,0:T(8,128)(2,1)S(1)}, bf16[224,512]{1,0:T(8,128)(2,1)S(1)}, u32[]{:S(2)}, u32[]{:S(2)}) collective-permute-start(bf16[224,512]{1,0:T(8,128)(2,1)S(1)} %get-tuple-element.35.refs_1_.mine_ref.refs_0_), channel_id=1, source_target_pairs={{0,4},{4,0},{8,12},{12,8},{16,20},{20,16},{24,28},{28,24},{1,5},{5... | collective-permute-start | bytes 688136 | tf_op jit(solution)/shard_map/ppermute | solution.py:328
  22.3 3.9 %collective-permute-start.10 = (bf16[224,512]{1,0:T(8,128)(2,1)S(1)}, bf16[224,512]{1,0:T(8,128)(2,1)S(1)}, u32[]{:S(2)}, u32[]{:S(2)}) collective-permute-start(bf16[224,512]{1,0:T(8,128)(2,1)S(1)} %collective-permute-done.9.refs_2_), channel_id=1, source_target_pairs={{0,4},{4,0},{8,12},{12,8},{16,20},{20,16},{24,28},{28,24},{1,5},{5... | collective-permute-start | bytes 688136 | tf_op jit(solution)/shard_map/ppermute | solution.py:328
  25.2 1.5 %collective-permute-start.12 = (bf16[224,512]{1,0:T(8,128)(2,1)S(1)}, bf16[224,512]{1,0:T(8,128)(2,1)S(1)}, u32[]{:S(2)}, u32[]{:S(2)}) collective-permute-start(bf16[224,512]{1,0:T(8,128)(2,1)S(1)} %collective-permute-done.11.refs_4_), channel_id=1, source_target_pairs={{0,4},{4,0},{8,12},{12,8},{16,20},{20,16},{24,28},{28,24},{1,5},{5... | collective-permute-start | bytes 688136 | tf_op jit(solution)/shard_map/ppermute | solution.py:328
  25.2 2.0 %collective-permute-start.7 = (bf16[224,512]{1,0:T(8,128)(2,1)S(1)}, bf16[224,512]{1,0:T(8,128)(2,1)S(1)}, u32[]{:S(2)}, u32[]{:S(2)}) collective-permute-start(bf16[224,512]{1,0:T(8,128)(2,1)S(1)} %shard_map.93.refs_0_), channel_id=1, source_target_pairs={{0,4},{4,0},{8,12},{12,8},{16,20},{20,16},{24,28},{28,24},{1,5},{5... | collective-permute-start | bytes 688136 | tf_op jit(solution)/shard_map/ppermute | solution.py:328
